TPU v7x, 32 devices: a whole 2x2x4 slice. The times are simulated.
32 devices in a mesh: groups: 2 (over y), hid: 4 (over z), wid: 4 (over x, core).
Axes of the slice: x: 2, y: 2, z: 4, core: 2. Of those that a mesh axis runs over, the one named last changes fastest.
Arguments:
- tokens: bfloat16 [1536, 12288], P(('groups', 'hid'), 'wid'), parts along dimension 0, may hold values from -6 to 6
- w_up: bfloat16 [12288, 24576], P('wid', 'hid'), may hold values from -0.0546875 to 0.0546875
- b_up: float32 [24576], P('hid'), may hold values from -4 to 4
- w_down: bfloat16 [24576, 12288], P('hid', 'wid'), may hold values from -0.0390625 to 0.0390625
- b_down: float32 [12288], P('wid'), may hold values from -3 to 3
Outputs:
- mixed: bfloat16 [1536, 12288], P(('groups', 'hid'), 'wid'), parts along dimension 0
There are 2 independent parts, one for each index of `groups`. A program takes and returns all parts, laid end to end along the dimension named above; an argument that names none is the same for every part. Nothing has to cross between parts.
All inputs are finite; a program needn't handle non-finite values.
Results may differ from a plain program's by a relative error of at most 0.0046.
Values may be sent and summed in bfloat16 or wider, within the bound.
A program may use at most 192 MiB of HBM per device.

v0:
```python
import jax
import jax.numpy as jnp
from jax import lax
from jax.sharding import PartitionSpec as P


def per_device(tokens, w_up, b_up, w_down, b_down):
    partial_pre = jnp.dot(
        lax.all_gather(tokens, "hid", axis=0, tiled=True), w_up, preferred_element_type=jnp.float32
    )
    share = lax.psum_scatter(partial_pre, "wid", scatter_dimension=0, tiled=True)
    local_hidden = jax.nn.gelu(share + b_up, approximate=True).astype(jnp.bfloat16)
    hidden = lax.all_gather(local_hidden, "wid", axis=0, tiled=True)
    summed_down = lax.psum_scatter(
        jnp.dot(hidden, w_down, preferred_element_type=jnp.float32),
        "hid",
        scatter_dimension=0,
        tiled=True,
    )
    return (summed_down + b_down).astype(jnp.bfloat16)


def solution(mesh):
    return jax.shard_map(
        per_device,
        mesh=mesh,
        in_specs=(
            P(("groups", "hid"), "wid"),
            P("wid", "hid"),
            P("hid"),
            P("hid", "wid"),
            P("wid"),
        ),
        out_specs=P(("groups", "hid"), "wid"),
        check_vma=False,
    )
```

profile of v0, /device:TPU:15, one launch (start us, length us, event | category | flops | bytes accessed | tf_op | source)
XLA Modules:
  0.0 552.0 jit_solution(5561964681493858263)
XLA Ops:
  6.5 0.0 all-gather.3.cloned.1.call-start
  6.5 0.7 all-gather.3.cloned.1.call-update
  7.3 0.0 reduce-scatter.3.cloned.1.call-start
  7.3 89.6 %all-gather.3.cloned.1.call-done = bf16[768,3072]{1,0:T(8,128)(2,1)} async-done(((bf16[192,3072]{1,0:T(8,128)(2,1)}), bf16[768,3072]{1,0:T(8,128)(2,1)}) %all-gather.3.cloned.1.call-update) | async-done | bytes 4718608 | tf_op jit(solution)/shard_map/all_gather | solution.py:9
  96.9 36.2 %fusion.8 = f32[768,6144]{1,0:T(8,128)} fusion(bf16[768,3072]{1,0:T(8,128)(2,1)} %all-gather.3.cloned.1.call-done, bf16[3072,6144]{1,0:T(8,128)(2,1)} %param.6), kind=kOutput, calls=%fused_computation.10 | convolution fusion | flops 28991029248 | bytes 61341696 | tf_op jit(solution)/shard_map/dot_general | solution.py:8
  133.1 0.0 copy-start
  133.1 0.0 reduce-scatter.3.cloned.1.call-update
  133.1 0.0 all-gather.5.cloned.1.call-start
  133.2 139.6 %reduce-scatter.3.cloned.1.call-done = f32[192,6144]{1,0:T(8,128)} async-done(((f32[768,6144]{1,0:T(8,128)}), f32[192,6144]{1,0:T(8,128)}) %reduce-scatter.3.cloned.1.call-update) | async-done | bytes 4718608 | tf_op jit(solution)/shard_map/reduce_scatter | solution.py:11
  272.8 0.0 copy-done
  272.8 5.3 fusion.7
  278.1 0.0 all-gather.5.cloned.1.call-update
  278.2 0.0 reduce-scatter.5.cloned.1.call-start
  278.2 64.8 %all-gather.5.cloned.1.call-done = bf16[768,6144]{1,0:T(8,128)(2,1)} async-done(((bf16[192,6144]{1,0:T(8,128)(2,1)}), bf16[768,6144]{1,0:T(8,128)(2,1)}) %all-gather.5.cloned.1.call-update) | async-done | bytes 9437200 | tf_op jit(solution)/shard_map/all_gather | solution.py:13
  343.0 37.8 %fusion.9 = f32[768,3072]{1,0:T(8,128)} fusion(bf16[768,6144]{1,0:T(8,128)(2,1)} %all-gather.5.cloned.1.call-done, bf16[6144,3072]{1,0:T(8,128)(2,1)} %param.8), kind=kOutput, calls=%fused_computation.11 | convolution fusion | flops 28991029248 | bytes 56623104 | tf_op jit(solution)/shard_map/dot_general | solution.py:15
  380.8 0.0 copy-start.1
  380.8 0.0 reduce-scatter.5.cloned.1.call-update
  380.8 161.8 %reduce-scatter.5.cloned.1.call-done = f32[192,3072]{1,0:T(8,128)} async-done(((f32[768,3072]{1,0:T(8,128)}), f32[192,3072]{1,0:T(8,128)}) %reduce-scatter.5.cloned.1.call-update) | async-done | bytes 2359312 | tf_op jit(solution)/shard_map/reduce_scatter | solution.py:14
  542.6 0.0 copy-done.1
  542.6 2.9 add_convert_fusion
Async XLA Ops:
  6.5 90.4 %all-gather.3.cloned.1.call-start = ((), (), s32[]{:S(2)}) async-start(), calls=%async_computation.2 | async-start | bytes 5898240 | tf_op jit(solution)/shard_map/all_gather | solution.py:9
  7.3 265.6 %reduce-scatter.3.cloned.1.call-start = ((), (), s32[]{:S(2)}) async-start(), calls=%async_computation.3 | async-start | bytes 23592960 | tf_op jit(solution)/shard_map/reduce_scatter | solution.py:11
  133.1 139.7 %copy-start = (f32[6144]{0:T(1024)S(1)}, f32[6144]{0:T(1024)}, u32[]{:S(2)}) copy-start(f32[6144]{0:T(1024)} %param.7) | copy-start | bytes 73732
  133.1 209.9 %all-gather.5.cloned.1.call-start = ((), (), s32[]{:S(2)}) async-start(), calls=%async_computation.4 | async-start | bytes 11796480 | tf_op jit(solution)/shard_map/all_gather | solution.py:13
  278.2 264.4 %reduce-scatter.5.cloned.1.call-start = ((), (), s32[]{:S(2)}) async-start(), calls=%async_computation.5 | async-start | bytes 11796480 | tf_op jit(solution)/shard_map/reduce_scatter | solution.py:14
  380.8 161.8 %copy-start.1 = (f32[3072]{0:T(1024)S(1)}, f32[3072]{0:T(1024)}, u32[]{:S(2)}) copy-start(f32[3072]{0:T(1024)} %param.9) | copy-start | bytes 36868
Sparse Core Ops, SparseCore 0:
  8.9 87.9 all-gather.2
  133.2 139.5 reduce-scatter.2
  278.3 64.6 all-gather.4
  380.9 161.6 reduce-scatter.4
where the time goes:
time: 554 us; the launch traced here: 552 us
  waiting for transfers between devices  457 us (82%)
  matrix products  73.9 us (13%)
  between operations  13.1 us (2%)
  other arithmetic  8.2 us (1%)
    reduce_scatter x1, waiting for transfers between devices, per_device(): lax.psum_scatter(jnp.dot(hidden, w_down, preferred_element_type=jnp.float...  162 us
    reduce_scatter x1, waiting for transfers between devices, per_device(): lax.psum_scatter(partial_pre, 'wid', scatter_dimension=0, tiled=True)  140 us
    all_gather x1, waiting for transfers between devices, per_device(): lax.all_gather(tokens, 'hid', axis=0, tiled=True)  89.6 us
    all_gather x1, waiting for transfers between devices, per_device(): hidden = lax.all_gather(local_hidden, 'wid', axis=0, tiled=True)  64.8 us
    dot_general x1, matrix products, per_device(): jnp.dot(hidden, w_down, preferred_element_type=jnp.float32)  37.8 us
    dot_general x1, matrix products, per_device(): jnp.dot(lax.all_gather(tokens, 'hid', axis=0, tiled=True), w_up, preferre...  36.2 us
  transfers between devices with their start and end apart: 4, of which 4 were waited for; matrix products, arithmetic and copies ran while one was open for 0% of the time, Pallas kernels for 0%

commit v1 on v0

v1 whole, which is shorter than its diff:
```python
import functools

import jax
import jax.numpy as jnp
from jax import lax
from jax.experimental import pallas as pl
from jax.experimental.pallas import tpu as pltpu
from jax.sharding import PartitionSpec as P

CHUNKS = 3
VMEM = 36 * 2**20
F32, BF16 = jnp.float32, jnp.bfloat16


def tile_of(columns, most):
    return max(t for t in range(128, most + 1, 128) if columns % t == 0)


def call(kernel, gates, args, specs, outs, grid, scratch, flops, nbytes):
    def body(*refs):
        kernel(*refs[len(gates):])
    return pl.pallas_call(
        body,
        grid=(grid,),
        in_specs=[pl.BlockSpec(memory_space=pl.ANY)] * len(gates) + specs,
        out_specs=[spec for spec, _ in outs],
        out_shape=[shape for _, shape in outs],
        scratch_shapes=scratch,
        compiler_params=pltpu.CompilerParams(vmem_limit_bytes=VMEM),
        cost_estimate=pl.CostEstimate(flops=flops, bytes_accessed=nbytes, transcendentals=0),
    )(*gates, *args)


def up(slots, w, gates):
    depth, columns = w.shape
    m = sum(s.shape[1] for s in slots)
    tile = tile_of(columns, 512)

    def kernel(*refs):
        slot_refs, (w_ref, own_ref, other_ref, lhs) = refs[:len(slots)], refs[len(slots):]

        @pl.when(pl.program_id(0) == 0)
        def _():
            for h in range(2):
                at = h * m
                for s in slot_refs:
                    lhs[at:at + s.shape[1], :] = s[h]
                    at += s.shape[1]
        pre = jnp.dot(lhs[...], w_ref[...], preferred_element_type=F32)
        own_ref[...] = pre[:m]
        other_ref[...] = pre[m:].astype(BF16)

    specs = [pl.BlockSpec(s.shape, lambda i: (0, 0, 0), pipeline_mode=pl.Buffered(1)) for s in slots]
    specs.append(pl.BlockSpec((depth, tile), lambda i: (0, i)))
    out = pl.BlockSpec((m, tile), lambda i: (0, i))
    return call(
        kernel, gates, [*slots, w], specs,
        [(out, jax.ShapeDtypeStruct((m, columns), F32)), (out, jax.ShapeDtypeStruct((m, columns), BF16))],
        columns // tile, [pltpu.VMEM((2 * m, depth), BF16)],
        4 * m * depth * columns, 2 * depth * columns + 6 * m * columns,
    )


def down(own, other, w, sizes, gates):
    m, depth = own.shape
    columns = w.shape[1]
    tile = tile_of(columns, 256)

    def kernel(own_ref, other_ref, w_ref, *rest):
        outs, lhs = rest[:-1], rest[-1]

        @pl.when(pl.program_id(0) == 0)
        def _():
            lhs[:m, :] = own_ref[...]
            lhs[m:, :] = other_ref[...]
        total = jnp.dot(lhs[...], w_ref[...], preferred_element_type=F32)
        for h in range(2):
            at = h * m
            for o in outs:
                o[h] = total[at:at + o.shape[1]].astype(o.dtype)
                at += o.shape[1]

    lhs_spec = pl.BlockSpec((m, depth), lambda i: (0, 0), pipeline_mode=pl.Buffered(1))
    specs = [lhs_spec, lhs_spec, pl.BlockSpec((depth, tile), lambda i: (0, i))]
    outs = [
        (pl.BlockSpec((2, r, tile), lambda i: (0, 0, i)),
         jax.ShapeDtypeStruct((2, r, columns), BF16 if j else F32))
        for j, r in enumerate(sizes)
    ]
    return call(
        kernel, gates, [own, other, w], specs, outs, columns // tile,
        [pltpu.VMEM((2 * m, depth), BF16)],
        4 * m * depth * columns, 2 * depth * columns + 4 * m * columns,
    )


def pointwise(f, args, bias, gates):
    m, columns = args[0].shape
    tile = tile_of(columns, 1536)
    arrays = list(args) + ([bias.reshape(1, -1)] if bias is not None else [])

    def kernel(*refs):
        refs[-1][...] = f(*[r[...].astype(F32) for r in refs[:-1]]).astype(BF16)

    specs = [pl.BlockSpec((a.shape[0], tile), lambda i: (0, i)) for a in arrays]
    return call(
        kernel, gates, arrays, specs,
        [(pl.BlockSpec((m, tile), lambda i: (0, i)), jax.ShapeDtypeStruct((m, columns), BF16))],
        columns // tile, [], 8 * m * columns, 10 * m * columns,
    )[0]


def activation(*terms):
    return jax.nn.gelu(functools.reduce(jnp.add, terms), approximate=True)


def make(n_hid, n_wid):
    chips = n_wid // 2
    sibling = [(i, i ^ 1) for i in range(n_wid)]

    def per_device(tokens, w_up, b_up, w_down, b_down):
        core = lax.rem(lax.axis_index("wid"), 2)
        rows = tokens.shape[0]
        half = rows // 2
        chunks = CHUNKS if half % CHUNKS == 0 else 1
        step = half // chunks
        apart = step % 16 == 0
        halves = tokens.reshape(2, half, -1)
        halves = jnp.where(core == 0, halves, halves[::-1])

        slots = []
        for k in range(chunks):
            block = halves[:, k * step:(k + 1) * step]
            if k:
                seen = sum(s[0, 0, 0].astype(F32) for s in slots[-1])
                block = jnp.where(jnp.isnan(seen), jnp.zeros_like(block), block)
            got = [block]
            for j in range(1, n_hid):
                got.append(lax.ppermute(block, "hid", [((i + j) % n_hid, i) for i in range(n_hid)]))
            slots.append(got)

        own, other, came, act, outs = {}, {}, {}, {}, {}
        last = []

        def run_up(k):
            nonlocal last
            lhs = slots[k] if apart else [jnp.concatenate(slots[k], axis=1)]
            ahead = [slots[k + 1][0]] if k + 1 < chunks else []
            own[k], mine = up(lhs, w_up, last + ahead)
            last = [mine]
            other[k] = lax.ppermute(mine, "wid", sibling)

        def run_across(k):
            nonlocal last
            send = pointwise(jnp.add, [own[k], other[k]], None, last)
            last = [send]
            came[k] = [
                lax.ppermute(send, "wid", [(i, (i + 2 * d) % n_wid) for i in range(n_wid)])
                for d in range(1, chips)
            ]

        def run_act(k):
            nonlocal last
            mine = pointwise(activation, [own[k], other[k], *came[k]], b_up, last)
            last = [mine]
            act[k] = (mine, lax.ppermute(mine, "wid", sibling))

        def run_down(k):
            nonlocal last
            sizes = [step] * n_hid if apart else [step * n_hid]
            parts = down(*act[k], w_down, sizes, last)
            last = [parts[-1]]
            if not apart:
                whole = parts[0]
                parts = [whole[:, j * step:(j + 1) * step] for j in range(n_hid)]
            total = parts[0]
            for j in range(1, n_hid):
                hops = [(i, (i + j) % n_hid) for i in range(n_hid)]
                total = total + lax.ppermute(parts[j].astype(BF16), "hid", hops).astype(F32)
            outs[k] = (total + b_down).astype(BF16)

        lag = 2
        for t in range(chunks + lag):
            if t < chunks:
                run_up(t)
            if t >= lag:
                run_act(t - lag)
            if t < chunks:
                run_across(t)
            if t >= lag:
                run_down(t - lag)
        out = jnp.concatenate([outs[k] for k in range(chunks)], axis=1)
        return jnp.where(core == 0, out, out[::-1]).reshape(rows, -1)

    return per_device


def solution(mesh):
    return jax.shard_map(
        make(mesh.shape["hid"], mesh.shape["wid"]),
        mesh=mesh,
        in_specs=(
            P(("groups", "hid"), "wid"),
            P("wid", "hid"),
            P("hid"),
            P("hid", "wid"),
            P("wid"),
        ),
        out_specs=P(("groups", "hid"), "wid"),
        check_vma=False,
    )
```

time: 554 us -> 364 us (0.66)
  waiting for transfers between devices: 457 us -> 188 us
  Pallas kernels: 0 us -> 124 us
  matrix products: 73.9 us -> 0 us
  starting transfers between devices: 0.12 us -> 34.7 us
  between operations: 13.1 us -> 5.25 us
    reduce_scatter x2 -> x0, waiting for transfers between devices: 301 us -> none  [the longest x1 162 us: per_device(): lax.psum_scatter(jnp.dot(hidden, w_down, preferred_element_type=jnp.float...]
    ppermute x0 -> x27, waiting for transfers between devices: none -> 188 us  [the longest x9 86.2 us: per_device(): lax.ppermute(block, 'hid', [((i + j) % n_hid, i) for i in range(n_hid)])]
    all_gather x2 -> x0, waiting for transfers between devices: 154 us -> none  [the longest x1 89.6 us: per_device(): lax.all_gather(tokens, 'hid', axis=0, tiled=True)]
    pallas_call x0 -> x12, Pallas kernels: none -> 124 us  [call(): pl.pallas_call(body, grid=(grid,), in_specs=[pl.BlockSpec(memory_space=pl...]
    dot_general x2 -> x0, matrix products: 73.9 us -> none  [the longest x1 37.8 us: per_device(): jnp.dot(hidden, w_down, preferred_element_type=jnp.float32)]
    ppermute x0 -> x27, starting transfers between devices: none -> 34.7 us  [the longest x9 13.7 us: per_device(): lax.ppermute(block, 'hid', [((i + j) % n_hid, i) for i in range(n_hid)])]
    convert_element_type x2 -> x1, other arithmetic: 8.2 us -> 0.71 us  [run_down(): outs[k] = (total + b_down).astype(BF16)]
  transfers between devices with their start and end apart: 4 -> 27, of which waited for: 4 -> 18; matrix products, arithmetic and copies ran while one was open for 0% -> 1% of each run, Pallas kernels for 0% -> 22%
where the time goes in v1:
time: 364 us; the launch traced here: 361 us
  waiting for transfers between devices  188 us (52%)
  Pallas kernels  124 us (34%)
  starting transfers between devices  34.7 us (10%)
  between operations  5.25 us (1%)
  other arithmetic  4.15 us (1%)
  local copies, waits for them, and re-layouts  4.11 us (1%)
    pallas_call x12, Pallas kernels, call(): pl.pallas_call(body, grid=(grid,), in_specs=[pl.BlockSpec(memory_space=pl...  124 us
    ppermute x9, waiting for transfers between devices, per_device(): lax.ppermute(block, 'hid', [((i + j) % n_hid, i) for i in range(n_hid)])  86.2 us
    ppermute x9, waiting for transfers between devices, run_down(): total = total + lax.ppermute(parts[j].astype(BF16), 'hid', hops).astype(F32)  72.4 us
    ppermute x3, waiting for transfers between devices, run_across(): lax.ppermute(send, 'wid', [(i, (i + 2 * d) % n_wid) for i in range(n_wid)])  26.4 us
    ppermute x9, starting transfers between devices, per_device(): lax.ppermute(block, 'hid', [((i + j) % n_hid, i) for i in range(n_hid)])  13.7 us
    ppermute x9, starting transfers between devices, run_down(): total = total + lax.ppermute(parts[j].astype(BF16), 'hid', hops).astype(F32)  12.8 us
  transfers between devices with their start and end apart: 27, of which 18 were waited for; matrix products, arithmetic and copies ran while one was open for 1% of the time, Pallas kernels for 22%

profile of v1, /device:TPU:15, one launch (start us, length us, event | category | flops | bytes accessed | tf_op | source)
XLA Modules:
  0.0 360.8 jit_solution(17450461813534201321)
XLA Ops:
  0.0 2.0 reverse_select_fusion.1
  2.1 0.2 collective-permute-start
  2.3 2.3 collective-permute-start.1
  4.6 2.2 collective-permute-start.2
  6.8 0.5 slice.45
  7.3 4.8 %collective-permute-done.refs_2_ = bf16[2,32,3072]{2,1,0:T(8,128)(2,1)S(1)} collective-permute-done((bf16[2,32,3072]{2,1,0:T(8,128)(2,1)S(1)}, bf16[2,32,3072]{2,1,0:T(8,128)(2,1)S(1)}, u32[]{:S(2)}, u32[]{:S(2)}) %collective-permute-start) | collective-permute-done | bytes 393248 | tf_op jit(solution)/shard_map/ppermute | solution.py:139
  12.1 0.5 slice.47
  13.8 15.7 %collective-permute-done.1.refs_3_ = bf16[2,32,3072]{2,1,0:T(8,128)(2,1)S(1)} collective-permute-done((bf16[2,32,3072]{2,1,0:T(8,128)(2,1)S(1)}, bf16[2,32,3072]{2,1,0:T(8,128)(2,1)S(1)}, u32[]{:S(2)}, u32[]{:S(2)}) %collective-permute-start.1) | collective-permute-done | bytes 393248 | tf_op jit(solution)/shard_map/ppermute | solution.py:139
  29.6 0.5 slice.48
  30.7 7.3 %collective-permute-done.2.refs_4_ = bf16[2,32,3072]{2,1,0:T(8,128)(2,1)S(1)} collective-permute-done((bf16[2,32,3072]{2,1,0:T(8,128)(2,1)S(1)}, bf16[2,32,3072]{2,1,0:T(8,128)(2,1)S(1)}, u32[]{:S(2)}, u32[]{:S(2)}) %collective-permute-start.2) | collective-permute-done | bytes 393248 | tf_op jit(solution)/shard_map/ppermute | solution.py:139
  38.0 0.5 slice.49
  39.2 19.3 %shard_map.55 = (f32[128,6144]{1,0:T(8,128)S(1)}, bf16[128,6144]{1,0:T(8,128)(2,1)S(1)}) custom-call(bf16[2,32,3072]{2,1,0:T(8,128)(2,1)S(1)} %slice_select_fusion.1.refs_0_.refs_2_, bf16[2,32,3072]{2,1,0:T(8,128)(2,1)S(1)} %slice.46.refs_1_, bf16[2,32,3072]{2,1,0:T(8,128)(2,1)S(1)} %collective-permute-done.refs_2_, ...), custom_call_target="tpu_custom_call" | custom-call | flops 9663676416 | bytes 42467328 | tf_op jit(solution)/shard_map/pallas_call | solution.py:22
  58.5 1.3 collective-permute-start.3
  59.8 2.0 collective-permute-start.4
  61.9 1.3 collective-permute-start.5
  63.2 0.5 slice.51
  63.7 7.7 %collective-permute-done.4.refs_3_ = bf16[2,32,3072]{2,1,0:T(8,128)(2,1)S(1)} collective-permute-done((bf16[2,32,3072]{2,1,0:T(8,128)(2,1)S(1)}, bf16[2,32,3072]{2,1,0:T(8,128)(2,1)S(1)}, u32[]{:S(2)}, u32[]{:S(2)}) %collective-permute-start.4) | collective-permute-done | bytes 393248 | tf_op jit(solution)/shard_map/ppermute | solution.py:139
  71.4 0.5 slice.52
  73.2 14.2 %collective-permute-done.5.refs_4_ = bf16[2,32,3072]{2,1,0:T(8,128)(2,1)S(1)} collective-permute-done((bf16[2,32,3072]{2,1,0:T(8,128)(2,1)S(1)}, bf16[2,32,3072]{2,1,0:T(8,128)(2,1)S(1)}, u32[]{:S(2)}, u32[]{:S(2)}) %collective-permute-start.5) | collective-permute-done | bytes 393248 | tf_op jit(solution)/shard_map/ppermute | solution.py:139
  87.3 0.5 slice.53
  88.5 7.3 %collective-permute-done.6.refs_5_ = bf16[2,32,3072]{2,1,0:T(8,128)(2,1)S(1)} collective-permute-done((bf16[2,32,3072]{2,1,0:T(8,128)(2,1)S(1)}, bf16[2,32,3072]{2,1,0:T(8,128)(2,1)S(1)}, u32[]{:S(2)}, u32[]{:S(2)}) %collective-permute-start.6) | collective-permute-done | bytes 393248 | tf_op jit(solution)/shard_map/ppermute | solution.py:139
  95.8 0.5 slice.54
  97.0 0.8 shard_map.56.refs_0_
  97.8 19.3 %shard_map.57 = (f32[128,6144]{1,0:T(8,128)S(1)}, bf16[128,6144]{1,0:T(8,128)(2,1)S(1)}) custom-call(bf16[128,6144]{1,0:T(8,128)(2,1)S(1)} %shard_map.56.refs_0_, bf16[2,32,3072]{2,1,0:T(8,128)(2,1)S(1)} %slice_select_fusion.refs_1_, bf16[2,32,3072]{2,1,0:T(8,128)(2,1)S(1)} %slice_select_fusion.1.refs_0_.refs_2_, ...), custom_call_target="tpu_custom_call" | custom-call | flops 9663676416 | bytes 42467328 | tf_op jit(solution)/shard_map/pallas_call | solution.py:22
  117.0 0.5 collective-permute-start.7
  117.6 0.3 collective-permute-start.11
  117.9 2.2 collective-permute-start.10
  120.0 1.3 collective-permute-start.8
  121.3 2.1 collective-permute-start.9
  123.4 0.8 shard_map.58.refs_0_
  124.2 6.3 %collective-permute-done.10.refs_4_ = bf16[2,32,3072]{2,1,0:T(8,128)(2,1)S(1)} collective-permute-done((bf16[2,32,3072]{2,1,0:T(8,128)(2,1)S(1)}, bf16[2,32,3072]{2,1,0:T(8,128)(2,1)S(1)}, u32[]{:S(2)}, u32[]{:S(2)}) %collective-permute-start.10) | collective-permute-done | bytes 393248 | tf_op jit(solution)/shard_map/ppermute | solution.py:139
  130.6 8.0 %collective-permute-done.8.refs_2_ = bf16[2,32,3072]{2,1,0:T(8,128)(2,1)S(1)} collective-permute-done((bf16[2,32,3072]{2,1,0:T(8,128)(2,1)S(1)}, bf16[2,32,3072]{2,1,0:T(8,128)(2,1)S(1)}, u32[]{:S(2)}, u32[]{:S(2)}) %collective-permute-start.8) | collective-permute-done | bytes 393248 | tf_op jit(solution)/shard_map/ppermute | solution.py:139
  138.5 15.0 %collective-permute-done.9.refs_3_ = bf16[2,32,3072]{2,1,0:T(8,128)(2,1)S(1)} collective-permute-done((bf16[2,32,3072]{2,1,0:T(8,128)(2,1)S(1)}, bf16[2,32,3072]{2,1,0:T(8,128)(2,1)S(1)}, u32[]{:S(2)}, u32[]{:S(2)}) %collective-permute-start.9) | collective-permute-done | bytes 393248 | tf_op jit(solution)/shard_map/ppermute | solution.py:139
  153.5 19.3 %shard_map.59 = (f32[128,6144]{1,0:T(8,128)S(1)}, bf16[128,6144]{1,0:T(8,128)(2,1)S(1)}) custom-call(bf16[128,6144]{1,0:T(8,128)(2,1)S(1)} %shard_map.58.refs_0_, bf16[2,32,3072]{2,1,0:T(8,128)(2,1)S(1)} %slice_select_fusion.refs_1_, bf16[2,32,3072]{2,1,0:T(8,128)(2,1)S(1)} %collective-permute-done.8.refs_2_, ...), custom_call_target="tpu_custom_call" | custom-call | flops 9663676416 | bytes 42467328 | tf_op jit(solution)/shard_map/pallas_call | solution.py:22
  172.7 1.2 collective-permute-start.12
  174.0 2.1 shard_map.60.refs_0_.refs_1_
  176.1 0.1 collective-permute-start.13
  176.2 1.2 collective-permute-start.17
  177.4 0.8 shard_map.61.refs_0_
  178.2 1.3 collective-permute-done.13.refs_2_
  179.5 19.4 %shard_map.62 = (f32[2,32,3072]{2,1,0:T(8,128)S(1)}, bf16[2,32,3072]{2,1,0:T(8,128)(2,1)S(1)}, bf16[2,32,3072]{2,1,0:T(8,128)(2,1)S(1)}, bf16[2,32,3072]{2,1,0:T(8,128)(2,1)S(1)}) custom-call(bf16[128,6144]{1,0:T(8,128)(2,1)S(1)} %shard_map.61.refs_0_, bf16[128,6144]{1,0:T(8,128)(2,1)S(1)} %shard_map.60.refs_0_.refs_1_, ...), custom_call_target="tpu_custom_call" | custom-call | flops 9663676416 | bytes 39321600 | tf_op jit(solution)/shard_map/pallas_call | solution.py:22
  198.9 12.8 %collective-permute-done.17.refs_3_ = bf16[128,6144]{1,0:T(8,128)(2,1)S(1)} collective-permute-done((bf16[128,6144]{1,0:T(8,128)(2,1)S(1)}, bf16[128,6144]{1,0:T(8,128)(2,1)S(1)}, u32[]{:S(2)}, u32[]{:S(2)}) %collective-permute-start.17) | collective-permute-done | bytes 1572896 | tf_op jit(solution)/shard_map/ppermute | solution.py:158
  211.8 2.1 shard_map.63.refs_0_.refs_1_
  213.8 1.3 collective-permute-start.18
  215.2 1.2 collective-permute-start.22
  216.4 1.8 collective-permute-done.18.refs_2_
  218.2 19.4 %shard_map.64 = (f32[2,32,3072]{2,1,0:T(8,128)S(1)}, bf16[2,32,3072]{2,1,0:T(8,128)(2,1)S(1)}, bf16[2,32,3072]{2,1,0:T(8,128)(2,1)S(1)}, bf16[2,32,3072]{2,1,0:T(8,128)(2,1)S(1)}) custom-call(bf16[128,6144]{1,0:T(8,128)(2,1)S(1)} %shard_map.63.refs_0_.refs_1_, bf16[128,6144]{1,0:T(8,128)(2,1)S(1)} %shard_map.63.refs_0_.refs_1_, ...), custom_call_target="tpu_custom_call" | custom-call | flops 9663676416 | bytes 39321600 | tf_op jit(solution)/shard_map/pallas_call | solution.py:22
  237.6 13.6 %collective-permute-done.22.refs_3_ = bf16[128,6144]{1,0:T(8,128)(2,1)S(1)} collective-permute-done((bf16[128,6144]{1,0:T(8,128)(2,1)S(1)}, bf16[128,6144]{1,0:T(8,128)(2,1)S(1)}, u32[]{:S(2)}, u32[]{:S(2)}) %collective-permute-start.22) | collective-permute-done | bytes 1572896 | tf_op jit(solution)/shard_map/ppermute | solution.py:158
  251.2 2.1 shard_map.65.refs_0_.refs_1_
  253.2 0.9 collective-permute-start.23
  254.1 3.4 collective-permute-start.16
  257.5 3.0 collective-permute-start.15
  260.5 1.5 collective-permute-start.19
  262.0 19.4 %shard_map.66 = (f32[2,32,3072]{2,1,0:T(8,128)S(1)}, bf16[2,32,3072]{2,1,0:T(8,128)(2,1)S(1)}, bf16[2,32,3072]{2,1,0:T(8,128)(2,1)S(1)}, bf16[2,32,3072]{2,1,0:T(8,128)(2,1)S(1)}) custom-call(bf16[128,6144]{1,0:T(8,128)(2,1)S(1)} %shard_map.65.refs_0_.refs_1_, bf16[128,6144]{1,0:T(8,128)(2,1)S(1)} %shard_map.65.refs_0_.refs_1_, ...), custom_call_target="tpu_custom_call" | custom-call | flops 9663676416 | bytes 39321600 | tf_op jit(solution)/shard_map/pallas_call | solution.py:22
  281.4 1.9 collective-permute-start.20
  283.2 16.5 %collective-permute-done.15 = bf16[2,32,3072]{2,1,0:T(8,128)(2,1)S(1)} collective-permute-done((bf16[2,32,3072]{2,1,0:T(8,128)(2,1)S(1)}, bf16[2,32,3072]{2,1,0:T(8,128)(2,1)S(1)}, u32[]{:S(2)}, u32[]{:S(2)}) %collective-permute-start.15) | collective-permute-done | bytes 393248 | tf_op jit(solution)/shard_map/ppermute | solution.py:179
  299.7 3.1 collective-permute-start.25
  302.8 13.7 %collective-permute-done.19 = bf16[2,32,3072]{2,1,0:T(8,128)(2,1)S(1)} collective-permute-done((bf16[2,32,3072]{2,1,0:T(8,128)(2,1)S(1)}, bf16[2,32,3072]{2,1,0:T(8,128)(2,1)S(1)}, u32[]{:S(2)}, u32[]{:S(2)}) %collective-permute-start.19) | collective-permute-done | bytes 393248 | tf_op jit(solution)/shard_map/ppermute | solution.py:179
  316.6 25.3 %collective-permute-done.20 = bf16[2,32,3072]{2,1,0:T(8,128)(2,1)S(1)} collective-permute-done((bf16[2,32,3072]{2,1,0:T(8,128)(2,1)S(1)}, bf16[2,32,3072]{2,1,0:T(8,128)(2,1)S(1)}, u32[]{:S(2)}, u32[]{:S(2)}) %collective-permute-start.20) | collective-permute-done | bytes 393248 | tf_op jit(solution)/shard_map/ppermute | solution.py:179
  341.9 8.4 %collective-permute-done.24 = bf16[2,32,3072]{2,1,0:T(8,128)(2,1)S(1)} collective-permute-done((bf16[2,32,3072]{2,1,0:T(8,128)(2,1)S(1)}, bf16[2,32,3072]{2,1,0:T(8,128)(2,1)S(1)}, u32[]{:S(2)}, u32[]{:S(2)}) %collective-permute-start.24) | collective-permute-done | bytes 393248 | tf_op jit(solution)/shard_map/ppermute | solution.py:179
  350.3 8.4 %collective-permute-done.25 = bf16[2,32,3072]{2,1,0:T(8,128)(2,1)S(1)} collective-permute-done((bf16[2,32,3072]{2,1,0:T(8,128)(2,1)S(1)}, bf16[2,32,3072]{2,1,0:T(8,128)(2,1)S(1)}, u32[]{:S(2)}, u32[]{:S(2)}) %collective-permute-start.25) | collective-permute-done | bytes 393248 | tf_op jit(solution)/shard_map/ppermute | solution.py:179
  358.7 0.7 add_convert_fusion.2
  359.4 0.1 pad_maximum_fusion
  359.5 1.3 reverse_select_fusion
  (21 shorter events, 0.1 us)
Async XLA Ops:
  2.1 10.0 %collective-permute-start = (bf16[2,32,3072]{2,1,0:T(8,128)(2,1)S(1)}, bf16[2,32,3072]{2,1,0:T(8,128)(2,1)S(1)}, u32[]{:S(2)}, u32[]{:S(2)}) collective-permute-start(bf16[2,32,3072]{2,1,0:T(8,128)(2,1)S(1)} %slice.46.refs_1_), channel_id=1, source_target_pairs={{4,0},{8,4},{12,8},{0,12},{5,1},{9,5},{13,9},{1,13},{6,2},{10,6},{... | collective-permute-start | bytes 1179656 | tf_op jit(solution)/shard_map/ppermute | solution.py:139
  2.3 27.3 %collective-permute-start.1 = (bf16[2,32,3072]{2,1,0:T(8,128)(2,1)S(1)}, bf16[2,32,3072]{2,1,0:T(8,128)(2,1)S(1)}, u32[]{:S(2)}, u32[]{:S(2)}) collective-permute-start(bf16[2,32,3072]{2,1,0:T(8,128)(2,1)S(1)} %slice.46.refs_1_), channel_id=1, source_target_pairs={{8,0},{12,4},{0,8},{4,12},{9,1},{13,5},{1,9},{5,13},{10,2},{14,6},... | collective-permute-start | bytes 1179656 | tf_op jit(solution)/shard_map/ppermute | solution.py:139
  4.6 33.4 %collective-permute-start.2 = (bf16[2,32,3072]{2,1,0:T(8,128)(2,1)S(1)}, bf16[2,32,3072]{2,1,0:T(8,128)(2,1)S(1)}, u32[]{:S(2)}, u32[]{:S(2)}) collective-permute-start(bf16[2,32,3072]{2,1,0:T(8,128)(2,1)S(1)} %slice.46.refs_1_), channel_id=1, source_target_pairs={{12,0},{0,4},{4,8},{8,12},{13,1},{1,5},{5,9},{9,13},{14,2},{2,6},{... | collective-permute-start | bytes 1179656 | tf_op jit(solution)/shard_map/ppermute | solution.py:139
  58.5 38.5 %collective-permute-start.3 = (bf16[128,6144]{1,0:T(8,128)(2,1)S(1)}, bf16[128,6144]{1,0:T(8,128)(2,1)S(1)}, u32[]{:S(2)}, u32[]{:S(2)}) collective-permute-start(bf16[128,6144]{1,0:T(8,128)(2,1)S(1)} %get-tuple-element.23.refs_0_), channel_id=1, source_target_pairs={{0,1},{1,0},{2,3},{3,2},{4,5},{5,4},{6,7},{7,6},{8,9},{9,8},{10,11... | collective-permute-start | bytes 4718600 | tf_op jit(solution)/shard_map/ppermute | solution.py:151
  59.8 11.6 %collective-permute-start.4 = (bf16[2,32,3072]{2,1,0:T(8,128)(2,1)S(1)}, bf16[2,32,3072]{2,1,0:T(8,128)(2,1)S(1)}, u32[]{:S(2)}, u32[]{:S(2)}) collective-permute-start(bf16[2,32,3072]{2,1,0:T(8,128)(2,1)S(1)} %slice_select_fusion.1.refs_0_.refs_2_), channel_id=1, source_target_pairs={{4,0},{8,4},{12,8},{0,12},{5,1},{9,5},{13,9},{1,13},{6,2},{10,6},{... | collective-permute-start | bytes 1179656 | tf_op jit(solution)/shard_map/ppermute | solution.py:139
  61.9 25.5 %collective-permute-start.5 = (bf16[2,32,3072]{2,1,0:T(8,128)(2,1)S(1)}, bf16[2,32,3072]{2,1,0:T(8,128)(2,1)S(1)}, u32[]{:S(2)}, u32[]{:S(2)}) collective-permute-start(bf16[2,32,3072]{2,1,0:T(8,128)(2,1)S(1)} %slice_select_fusion.1.refs_0_.refs_2_), channel_id=1, source_target_pairs={{8,0},{12,4},{0,8},{4,12},{9,1},{13,5},{1,9},{5,13},{10,2},{14,6},... | collective-permute-start | bytes 1179656 | tf_op jit(solution)/shard_map/ppermute | solution.py:139
  63.2 32.6 %collective-permute-start.6 = (bf16[2,32,3072]{2,1,0:T(8,128)(2,1)S(1)}, bf16[2,32,3072]{2,1,0:T(8,128)(2,1)S(1)}, u32[]{:S(2)}, u32[]{:S(2)}) collective-permute-start(bf16[2,32,3072]{2,1,0:T(8,128)(2,1)S(1)} %slice_select_fusion.1.refs_0_.refs_2_), channel_id=1, source_target_pairs={{12,0},{0,4},{4,8},{8,12},{13,1},{1,5},{5,9},{9,13},{14,2},{2,6},{... | collective-permute-start | bytes 1179656 | tf_op jit(solution)/shard_map/ppermute | solution.py:139
  117.0 6.4 %collective-permute-start.7 = (bf16[128,6144]{1,0:T(8,128)(2,1)S(1)}, bf16[128,6144]{1,0:T(8,128)(2,1)S(1)}, u32[]{:S(2)}, u32[]{:S(2)}) collective-permute-start(bf16[128,6144]{1,0:T(8,128)(2,1)S(1)} %get-tuple-element.25.refs_0_), channel_id=1, source_target_pairs={{0,1},{1,0},{2,3},{3,2},{4,5},{5,4},{6,7},{7,6},{8,9},{9,8},{10,11... | collective-permute-start | bytes 4718600 | tf_op jit(solution)/shard_map/ppermute | solution.py:151
  117.6 56.4 %collective-permute-start.11 = (bf16[128,6144]{1,0:T(8,128)(2,1)S(1)}, bf16[128,6144]{1,0:T(8,128)(2,1)S(1)}, u32[]{:S(2)}, u32[]{:S(2)}) collective-permute-start(bf16[128,6144]{1,0:T(8,128)(2,1)S(1)} %shard_map.56.refs_0_), channel_id=1, source_target_pairs={{0,2},{1,3},{2,0},{3,1},{4,6},{5,7},{6,4},{7,5},{8,10},{9,11},{10,... | collective-permute-start | bytes 4718600 | tf_op jit(solution)/shard_map/ppermute | solution.py:158
  117.9 12.7 %collective-permute-start.10 = (bf16[2,32,3072]{2,1,0:T(8,128)(2,1)S(1)}, bf16[2,32,3072]{2,1,0:T(8,128)(2,1)S(1)}, u32[]{:S(2)}, u32[]{:S(2)}) collective-permute-start(bf16[2,32,3072]{2,1,0:T(8,128)(2,1)S(1)} %slice_select_fusion.refs_1_), channel_id=1, source_target_pairs={{12,0},{0,4},{4,8},{8,12},{13,1},{1,5},{5,9},{9,13},{14,2},{2,6},{... | collective-permute-start | bytes 1179656 | tf_op jit(solution)/shard_map/ppermute | solution.py:139
  120.0 18.5 %collective-permute-start.8 = (bf16[2,32,3072]{2,1,0:T(8,128)(2,1)S(1)}, bf16[2,32,3072]{2,1,0:T(8,128)(2,1)S(1)}, u32[]{:S(2)}, u32[]{:S(2)}) collective-permute-start(bf16[2,32,3072]{2,1,0:T(8,128)(2,1)S(1)} %slice_select_fusion.refs_1_), channel_id=1, source_target_pairs={{4,0},{8,4},{12,8},{0,12},{5,1},{9,5},{13,9},{1,13},{6,2},{10,6},{... | collective-permute-start | bytes 1179656 | tf_op jit(solution)/shard_map/ppermute | solution.py:139
  121.3 32.1 %collective-permute-start.9 = (bf16[2,32,3072]{2,1,0:T(8,128)(2,1)S(1)}, bf16[2,32,3072]{2,1,0:T(8,128)(2,1)S(1)}, u32[]{:S(2)}, u32[]{:S(2)}) collective-permute-start(bf16[2,32,3072]{2,1,0:T(8,128)(2,1)S(1)} %slice_select_fusion.refs_1_), channel_id=1, source_target_pairs={{8,0},{12,4},{0,8},{4,12},{9,1},{13,5},{1,9},{5,13},{10,2},{14,6},... | collective-permute-start | bytes 1179656 | tf_op jit(solution)/shard_map/ppermute | solution.py:139
  124.2 49.8 %copy-start = (f32[6144]{0:T(1024)S(1)}, f32[6144]{0:T(1024)}, u32[]{:S(2)}) copy-start(f32[6144]{0:T(1024)} %param.7) | copy-start | bytes 73732
  172.7 4.7 %collective-permute-start.12 = (bf16[128,6144]{1,0:T(8,128)(2,1)S(1)}, bf16[128,6144]{1,0:T(8,128)(2,1)S(1)}, u32[]{:S(2)}, u32[]{:S(2)}) collective-permute-start(bf16[128,6144]{1,0:T(8,128)(2,1)S(1)} %get-tuple-element.27.refs_0_), channel_id=1, source_target_pairs={{0,1},{1,0},{2,3},{3,2},{4,5},{5,4},{6,7},{7,6},{8,9},{9,8},{10,11... | collective-permute-start | bytes 4718600 | tf_op jit(solution)/shard_map/ppermute | solution.py:151
  176.1 3.5 collective-permute-start.13
  176.2 35.6 %collective-permute-start.17 = (bf16[128,6144]{1,0:T(8,128)(2,1)S(1)}, bf16[128,6144]{1,0:T(8,128)(2,1)S(1)}, u32[]{:S(2)}, u32[]{:S(2)}) collective-permute-start(bf16[128,6144]{1,0:T(8,128)(2,1)S(1)} %shard_map.58.refs_0_), channel_id=1, source_target_pairs={{0,2},{1,3},{2,0},{3,1},{4,6},{5,7},{6,4},{7,5},{8,10},{9,11},{10,... | collective-permute-start | bytes 4718600 | tf_op jit(solution)/shard_map/ppermute | solution.py:158
  213.8 4.4 %collective-permute-start.18 = (bf16[128,6144]{1,0:T(8,128)(2,1)S(1)}, bf16[128,6144]{1,0:T(8,128)(2,1)S(1)}, u32[]{:S(2)}, u32[]{:S(2)}) collective-permute-start(bf16[128,6144]{1,0:T(8,128)(2,1)S(1)} %shard_map.63.refs_0_.refs_1_), channel_id=1, source_target_pairs={{0,1},{1,0},{2,3},{3,2},{4,5},{5,4},{6,7},{7,6},{8,9},{9,8},{10,11... | collective-permute-start | bytes 4718600 | tf_op jit(solution)/shard_map/ppermute | solution.py:166
  215.2 36.0 %collective-permute-start.22 = (bf16[128,6144]{1,0:T(8,128)(2,1)S(1)}, bf16[128,6144]{1,0:T(8,128)(2,1)S(1)}, u32[]{:S(2)}, u32[]{:S(2)}) collective-permute-start(bf16[128,6144]{1,0:T(8,128)(2,1)S(1)} %shard_map.61.refs_0_), channel_id=1, source_target_pairs={{0,2},{1,3},{2,0},{3,1},{4,6},{5,7},{6,4},{7,5},{8,10},{9,11},{10,... | collective-permute-start | bytes 4718600 | tf_op jit(solution)/shard_map/ppermute | solution.py:158
  253.2 7.3 %collective-permute-start.23 = (bf16[128,6144]{1,0:T(8,128)(2,1)S(1)}, bf16[128,6144]{1,0:T(8,128)(2,1)S(1)}, u32[]{:S(2)}, u32[]{:S(2)}) collective-permute-start(bf16[128,6144]{1,0:T(8,128)(2,1)S(1)} %shard_map.65.refs_0_.refs_1_), channel_id=1, source_target_pairs={{0,1},{1,0},{2,3},{3,2},{4,5},{5,4},{6,7},{7,6},{8,9},{9,8},{10,11... | collective-permute-start | bytes 4718600 | tf_op jit(solution)/shard_map/ppermute | solution.py:166
  254.1 45.6 %collective-permute-start.16 = (bf16[2,32,3072]{2,1,0:T(8,128)(2,1)S(1)}, bf16[2,32,3072]{2,1,0:T(8,128)(2,1)S(1)}, u32[]{:S(2)}, u32[]{:S(2)}) collective-permute-start(bf16[2,32,3072]{2,1,0:T(8,128)(2,1)S(1)} %get-tuple-element.32.refs_0_), channel_id=1, source_target_pairs={{0,12},{4,0},{8,4},{12,8},{1,13},{5,1},{9,5},{13,9},{2,14},{6,2},{... | collective-permute-start | bytes 1179656 | tf_op jit(solution)/shard_map/ppermute | solution.py:179
  257.5 23.8 %collective-permute-start.14 = (bf16[2,32,3072]{2,1,0:T(8,128)(2,1)S(1)}, bf16[2,32,3072]{2,1,0:T(8,128)(2,1)S(1)}, u32[]{:S(2)}, u32[]{:S(2)}) collective-permute-start(bf16[2,32,3072]{2,1,0:T(8,128)(2,1)S(1)} %get-tuple-element.30), channel_id=1, source_target_pairs={{0,4},{4,8},{8,12},{12,0},{1,5},{5,9},{9,13},{13,1},{2,6},{6,10},{... | collective-permute-start | bytes 1179656 | tf_op jit(solution)/shard_map/ppermute | solution.py:179
  257.5 42.2 %collective-permute-start.15 = (bf16[2,32,3072]{2,1,0:T(8,128)(2,1)S(1)}, bf16[2,32,3072]{2,1,0:T(8,128)(2,1)S(1)}, u32[]{:S(2)}, u32[]{:S(2)}) collective-permute-start(bf16[2,32,3072]{2,1,0:T(8,128)(2,1)S(1)} %get-tuple-element.31), channel_id=1, source_target_pairs={{0,8},{4,12},{8,0},{12,4},{1,9},{5,13},{9,1},{13,5},{2,10},{6,14},... | collective-permute-start | bytes 1179656 | tf_op jit(solution)/shard_map/ppermute | solution.py:179
  260.5 81.3 %collective-permute-start.21 = (bf16[2,32,3072]{2,1,0:T(8,128)(2,1)S(1)}, bf16[2,32,3072]{2,1,0:T(8,128)(2,1)S(1)}, u32[]{:S(2)}, u32[]{:S(2)}) collective-permute-start(bf16[2,32,3072]{2,1,0:T(8,128)(2,1)S(1)} %get-tuple-element.36.refs_0_), channel_id=1, source_target_pairs={{0,12},{4,0},{8,4},{12,8},{1,13},{5,1},{9,5},{13,9},{2,14},{6,2},{... | collective-permute-start | bytes 1179656 | tf_op jit(solution)/shard_map/ppermute | solution.py:179
  260.5 98.2 %copy-start.1 = (f32[3072]{0:T(1024)S(1)}, f32[3072]{0:T(1024)}, u32[]{:S(2)}) copy-start(f32[3072]{0:T(1024)} %param.9) | copy-start | bytes 36868
  260.5 56.0 %collective-permute-start.19 = (bf16[2,32,3072]{2,1,0:T(8,128)(2,1)S(1)}, bf16[2,32,3072]{2,1,0:T(8,128)(2,1)S(1)}, u32[]{:S(2)}, u32[]{:S(2)}) collective-permute-start(bf16[2,32,3072]{2,1,0:T(8,128)(2,1)S(1)} %get-tuple-element.34), channel_id=1, source_target_pairs={{0,4},{4,8},{8,12},{12,0},{1,5},{5,9},{9,13},{13,1},{2,6},{6,10},{... | collective-permute-start | bytes 1179656 | tf_op jit(solution)/shard_map/ppermute | solution.py:179
  281.4 60.5 %collective-permute-start.20 = (bf16[2,32,3072]{2,1,0:T(8,128)(2,1)S(1)}, bf16[2,32,3072]{2,1,0:T(8,128)(2,1)S(1)}, u32[]{:S(2)}, u32[]{:S(2)}) collective-permute-start(bf16[2,32,3072]{2,1,0:T(8,128)(2,1)S(1)} %get-tuple-element.35), channel_id=1, source_target_pairs={{0,8},{4,12},{8,0},{12,4},{1,9},{5,13},{9,1},{13,5},{2,10},{6,14},... | collective-permute-start | bytes 1179656 | tf_op jit(solution)/shard_map/ppermute | solution.py:179
  299.7 50.6 %collective-permute-start.24 = (bf16[2,32,3072]{2,1,0:T(8,128)(2,1)S(1)}, bf16[2,32,3072]{2,1,0:T(8,128)(2,1)S(1)}, u32[]{:S(2)}, u32[]{:S(2)}) collective-permute-start(bf16[2,32,3072]{2,1,0:T(8,128)(2,1)S(1)} %get-tuple-element.38), channel_id=1, source_target_pairs={{0,4},{4,8},{8,12},{12,0},{1,5},{5,9},{9,13},{13,1},{2,6},{6,10},{... | collective-permute-start | bytes 1179656 | tf_op jit(solution)/shard_map/ppermute | solution.py:179
  299.7 59.0 %collective-permute-start.25 = (bf16[2,32,3072]{2,1,0:T(8,128)(2,1)S(1)}, bf16[2,32,3072]{2,1,0:T(8,128)(2,1)S(1)}, u32[]{:S(2)}, u32[]{:S(2)}) collective-permute-start(bf16[2,32,3072]{2,1,0:T(8,128)(2,1)S(1)} %get-tuple-element.39), channel_id=1, source_target_pairs={{0,8},{4,12},{8,0},{12,4},{1,9},{5,13},{9,1},{13,5},{2,10},{6,14},... | collective-permute-start | bytes 1179656 | tf_op jit(solution)/shard_map/ppermute | solution.py:179
  316.6 42.1 %collective-permute-start.26 = (bf16[2,32,3072]{2,1,0:T(8,128)(2,1)S(1)}, bf16[2,32,3072]{2,1,0:T(8,128)(2,1)S(1)}, u32[]{:S(2)}, u32[]{:S(2)}) collective-permute-start(bf16[2,32,3072]{2,1,0:T(8,128)(2,1)S(1)} %get-tuple-element.40), channel_id=1, source_target_pairs={{0,12},{4,0},{8,4},{12,8},{1,13},{5,1},{9,5},{13,9},{2,14},{6,2},{... | collective-permute-start | bytes 1179656 | tf_op jit(solution)/shard_map/ppermute | solution.py:179

commit v2 on v1

--- a/solution.py
+++ b/solution.py
@@ -16,7 +16,7 @@
     return max(t for t in range(128, most + 1, 128) if columns % t == 0)
 
 
-def call(kernel, gates, args, specs, outs, grid, scratch, flops, nbytes):
+def call(kernel, gates, args, specs, outs, grid, scratch):
     def body(*refs):
         kernel(*refs[len(gates):])
     return pl.pallas_call(
@@ -27,7 +27,7 @@
         out_shape=[shape for _, shape in outs],
         scratch_shapes=scratch,
         compiler_params=pltpu.CompilerParams(vmem_limit_bytes=VMEM),
-        cost_estimate=pl.CostEstimate(flops=flops, bytes_accessed=nbytes, transcendentals=0),
+        cost_estimate=pl.CostEstimate(flops=1024, bytes_accessed=1024, transcendentals=0),
     )(*gates, *args)
 
 
@@ -57,7 +57,6 @@
         kernel, gates, [*slots, w], specs,
         [(out, jax.ShapeDtypeStruct((m, columns), F32)), (out, jax.ShapeDtypeStruct((m, columns), BF16))],
         columns // tile, [pltpu.VMEM((2 * m, depth), BF16)],
-        4 * m * depth * columns, 2 * depth * columns + 6 * m * columns,
     )
 
 
@@ -90,7 +89,6 @@
     return call(
         kernel, gates, [own, other, w], specs, outs, columns // tile,
         [pltpu.VMEM((2 * m, depth), BF16)],
-        4 * m * depth * columns, 2 * depth * columns + 4 * m * columns,
     )
 
 
@@ -106,7 +104,7 @@
     return call(
         kernel, gates, arrays, specs,
         [(pl.BlockSpec((m, tile), lambda i: (0, i)), jax.ShapeDtypeStruct((m, columns), BF16))],
-        columns // tile, [], 8 * m * columns, 10 * m * columns,
+        columns // tile, [],
     )[0]
 
 
@@ -139,7 +137,7 @@
                 got.append(lax.ppermute(block, "hid", [((i + j) % n_hid, i) for i in range(n_hid)]))
             slots.append(got)
 
-        own, other, came, act, outs = {}, {}, {}, {}, {}
+        own, other, came, act, far, outs = {}, {}, {}, {}, {}, {}
         last = []
 
         def run_up(k):
@@ -161,25 +159,29 @@
 
         def run_act(k):
             nonlocal last
-            mine = pointwise(activation, [own[k], other[k], *came[k]], b_up, last)
+            settled = far[k - 2] if k >= 2 else []
+            mine = pointwise(activation, [own[k], other[k], *came[k]], b_up, last + settled)
             last = [mine]
             act[k] = (mine, lax.ppermute(mine, "wid", sibling))
 
         def run_down(k):
             nonlocal last
             sizes = [step] * n_hid if apart else [step * n_hid]
-            parts = down(*act[k], w_down, sizes, last)
+            settled = far[k - 1][:1] if 0 < k == chunks - 1 else []
+            parts = down(*act[k], w_down, sizes, last + settled)
             last = [parts[-1]]
             if not apart:
                 whole = parts[0]
                 parts = [whole[:, j * step:(j + 1) * step] for j in range(n_hid)]
             total = parts[0]
+            far[k] = []
             for j in range(1, n_hid):
                 hops = [(i, (i + j) % n_hid) for i in range(n_hid)]
-                total = total + lax.ppermute(parts[j].astype(BF16), "hid", hops).astype(F32)
+                far[k].append(lax.ppermute(parts[j].astype(BF16), "hid", hops))
+                total = total + far[k][-1].astype(F32)
             outs[k] = (total + b_down).astype(BF16)
 
-        lag = 2
+        lag = 1
         for t in range(chunks + lag):
             if t < chunks:
                 run_up(t)

time: 364 us -> 306 us (0.84)
  waiting for transfers between devices: 188 us -> 127 us
  starting transfers between devices: 34.7 us -> 39 us
    ppermute x3, waiting for transfers between devices: 26.4 us -> 0.01 us  [run_across(): lax.ppermute(send, 'wid', [(i, (i + 2 * d) % n_wid) for i in range(n_wid)])]
    ppermute x9, waiting for transfers between devices: 86.2 us -> 68.1 us  [per_device(): lax.ppermute(block, 'hid', [((i + j) % n_hid, i) for i in range(n_hid)])]
    ppermute x9, waiting for transfers between devices: 72.4 us -> 55.2 us  [run_down(): far[k].append(lax.ppermute(parts[j].astype(BF16), 'hid', hops))]
    ppermute x9, starting transfers between devices: 12.8 us -> 19.7 us  [run_down(): far[k].append(lax.ppermute(parts[j].astype(BF16), 'hid', hops))]
    ppermute x3, waiting for transfers between devices: 0.01 us -> 3.89 us  [run_up(): other[k] = lax.ppermute(mine, 'wid', sibling)]
  transfers between devices with their start and end apart: 27 -> 27, of which waited for: 18 -> 16; matrix products, arithmetic and copies ran while one was open for 1% -> 1% of each run, Pallas kernels for 22% -> 34%
where the time goes in v2:
time: 306 us; the launch traced here: 304 us
  waiting for transfers between devices  127 us (42%)
  Pallas kernels  124 us (41%)
  starting transfers between devices  39 us (13%)
  between operations  5.25 us (2%)
  other arithmetic  4.17 us (1%)
  local copies, waits for them, and re-layouts  4.11 us (1%)
    pallas_call x12, Pallas kernels, call(): pl.pallas_call(body, grid=(grid,), in_specs=[pl.BlockSpec(memory_space=pl...  124 us
    ppermute x9, waiting for transfers between devices, per_device(): lax.ppermute(block, 'hid', [((i + j) % n_hid, i) for i in range(n_hid)])  68.1 us
    ppermute x9, waiting for transfers between devices, run_down(): far[k].append(lax.ppermute(parts[j].astype(BF16), 'hid', hops))  55.2 us
    ppermute x9, starting transfers between devices, run_down(): far[k].append(lax.ppermute(parts[j].astype(BF16), 'hid', hops))  19.7 us
    ppermute x9, starting transfers between devices, per_device(): lax.ppermute(block, 'hid', [((i + j) % n_hid, i) for i in range(n_hid)])  12.9 us
  transfers between devices with their start and end apart: 27, of which 16 were waited for; matrix products, arithmetic and copies ran while one was open for 1% of the time, Pallas kernels for 34%

profile of v2, /device:TPU:15, one launch (start us, length us, event | category | flops | bytes accessed | tf_op | source)
XLA Modules:
  0.0 304.2 jit_solution(9154697498696027208)
XLA Ops:
  0.0 2.0 reverse_select_fusion.1
  2.1 0.2 collective-permute-start
  2.3 2.3 collective-permute-start.1
  4.6 2.2 collective-permute-start.2
  6.8 0.5 slice.45
  7.3 4.8 %collective-permute-done.refs_2_ = bf16[2,32,3072]{2,1,0:T(8,128)(2,1)S(1)} collective-permute-done((bf16[2,32,3072]{2,1,0:T(8,128)(2,1)S(1)}, bf16[2,32,3072]{2,1,0:T(8,128)(2,1)S(1)}, u32[]{:S(2)}, u32[]{:S(2)}) %collective-permute-start) | collective-permute-done | bytes 393248 | tf_op jit(solution)/shard_map/ppermute | solution.py:137
  12.1 0.5 slice.47
  13.8 15.7 %collective-permute-done.1.refs_3_ = bf16[2,32,3072]{2,1,0:T(8,128)(2,1)S(1)} collective-permute-done((bf16[2,32,3072]{2,1,0:T(8,128)(2,1)S(1)}, bf16[2,32,3072]{2,1,0:T(8,128)(2,1)S(1)}, u32[]{:S(2)}, u32[]{:S(2)}) %collective-permute-start.1) | collective-permute-done | bytes 393248 | tf_op jit(solution)/shard_map/ppermute | solution.py:137
  29.6 0.5 slice.48
  30.7 7.3 %collective-permute-done.2.refs_4_ = bf16[2,32,3072]{2,1,0:T(8,128)(2,1)S(1)} collective-permute-done((bf16[2,32,3072]{2,1,0:T(8,128)(2,1)S(1)}, bf16[2,32,3072]{2,1,0:T(8,128)(2,1)S(1)}, u32[]{:S(2)}, u32[]{:S(2)}) %collective-permute-start.2) | collective-permute-done | bytes 393248 | tf_op jit(solution)/shard_map/ppermute | solution.py:137
  38.0 0.5 slice.49
  39.2 19.3 %shard_map.55 = (f32[128,6144]{1,0:T(8,128)S(1)}, bf16[128,6144]{1,0:T(8,128)(2,1)S(1)}) custom-call(bf16[2,32,3072]{2,1,0:T(8,128)(2,1)S(1)} %slice_select_fusion.1.refs_0_.refs_2_, bf16[2,32,3072]{2,1,0:T(8,128)(2,1)S(1)} %slice.46.refs_1_, bf16[2,32,3072]{2,1,0:T(8,128)(2,1)S(1)} %collective-permute-done.refs_2_, ...), custom_call_target="tpu_custom_call" | custom-call | flops 1024 | bytes 1024 | tf_op jit(solution)/shard_map/pallas_call | solution.py:22
  58.5 1.3 collective-permute-start.3
  59.8 3.0 collective-permute-done.3.refs_2_
  62.9 0.8 shard_map.56.refs_0_
  63.6 0.3 collective-permute-start.7
  63.9 2.0 collective-permute-start.4
  66.0 1.3 collective-permute-start.5
  67.3 0.5 slice.51
  67.8 7.2 %collective-permute-done.4.refs_3_ = bf16[2,32,3072]{2,1,0:T(8,128)(2,1)S(1)} collective-permute-done((bf16[2,32,3072]{2,1,0:T(8,128)(2,1)S(1)}, bf16[2,32,3072]{2,1,0:T(8,128)(2,1)S(1)}, u32[]{:S(2)}, u32[]{:S(2)}) %collective-permute-start.4) | collective-permute-done | bytes 393248 | tf_op jit(solution)/shard_map/ppermute | solution.py:137
  75.0 0.5 slice.52
  76.7 14.7 %collective-permute-done.5.refs_4_ = bf16[2,32,3072]{2,1,0:T(8,128)(2,1)S(1)} collective-permute-done((bf16[2,32,3072]{2,1,0:T(8,128)(2,1)S(1)}, bf16[2,32,3072]{2,1,0:T(8,128)(2,1)S(1)}, u32[]{:S(2)}, u32[]{:S(2)}) %collective-permute-start.5) | collective-permute-done | bytes 393248 | tf_op jit(solution)/shard_map/ppermute | solution.py:137
  91.4 0.5 slice.53
  92.6 7.3 %collective-permute-done.6.refs_5_ = bf16[2,32,3072]{2,1,0:T(8,128)(2,1)S(1)} collective-permute-done((bf16[2,32,3072]{2,1,0:T(8,128)(2,1)S(1)}, bf16[2,32,3072]{2,1,0:T(8,128)(2,1)S(1)}, u32[]{:S(2)}, u32[]{:S(2)}) %collective-permute-start.6) | collective-permute-done | bytes 393248 | tf_op jit(solution)/shard_map/ppermute | solution.py:137
  99.9 0.5 slice.54
  101.1 19.3 %shard_map.57 = (f32[128,6144]{1,0:T(8,128)S(1)}, bf16[128,6144]{1,0:T(8,128)(2,1)S(1)}) custom-call(bf16[128,6144]{1,0:T(8,128)(2,1)S(1)} %shard_map.56.refs_0_, bf16[2,32,3072]{2,1,0:T(8,128)(2,1)S(1)} %slice_select_fusion.refs_1_, bf16[2,32,3072]{2,1,0:T(8,128)(2,1)S(1)} %slice_select_fusion.1.refs_0_.refs_2_, ...), custom_call_target="tpu_custom_call" | custom-call | flops 1024 | bytes 1024 | tf_op jit(solution)/shard_map/pallas_call | solution.py:22
  120.4 0.6 collective-permute-start.8
  120.9 2.1 shard_map.58.refs_0_.refs_1_
  123.0 0.1 collective-permute-start.9
  123.1 3.5 %collective-permute-start.13 = (bf16[2,32,3072]{2,1,0:T(8,128)(2,1)S(1)}, bf16[2,32,3072]{2,1,0:T(8,128)(2,1)S(1)}, u32[]{:S(2)}, u32[]{:S(2)}) collective-permute-start(bf16[2,32,3072]{2,1,0:T(8,128)(2,1)S(1)} %slice_select_fusion.refs_1_), channel_id=1, source_target_pairs={{4,0},{8,4},{12,8},{0,12},{5,1},{9,5},{13,9},{1,13},{6,2},{10,6},{... | collective-permute-start | bytes 1179656 | tf_op jit(solution)/shard_map/ppermute | solution.py:137
  126.6 1.3 collective-permute-start.15
  127.9 0.8 shard_map.59.refs_0_
  128.7 1.3 collective-permute-start.16
  130.0 19.4 %shard_map.60 = (f32[2,32,3072]{2,1,0:T(8,128)S(1)}, bf16[2,32,3072]{2,1,0:T(8,128)(2,1)S(1)}, bf16[2,32,3072]{2,1,0:T(8,128)(2,1)S(1)}, bf16[2,32,3072]{2,1,0:T(8,128)(2,1)S(1)}) custom-call(bf16[128,6144]{1,0:T(8,128)(2,1)S(1)} %shard_map.59.refs_0_, bf16[128,6144]{1,0:T(8,128)(2,1)S(1)} %shard_map.58.refs_0_.refs_1_, ...), custom_call_target="tpu_custom_call" | custom-call | flops 1024 | bytes 1024 | tf_op jit(solution)/shard_map/pallas_call | solution.py:22
  149.3 2.8 collective-permute-done.14.refs_3_
  152.1 8.4 %collective-permute-done.15.refs_4_ = bf16[2,32,3072]{2,1,0:T(8,128)(2,1)S(1)} collective-permute-done((bf16[2,32,3072]{2,1,0:T(8,128)(2,1)S(1)}, bf16[2,32,3072]{2,1,0:T(8,128)(2,1)S(1)}, u32[]{:S(2)}, u32[]{:S(2)}) %collective-permute-start.15) | collective-permute-done | bytes 393248 | tf_op jit(solution)/shard_map/ppermute | solution.py:137
  160.5 19.3 %shard_map.61 = (f32[128,6144]{1,0:T(8,128)S(1)}, bf16[128,6144]{1,0:T(8,128)(2,1)S(1)}) custom-call(bf16[2,32,3072]{2,1,0:T(8,128)(2,1)S(1)} %get-tuple-element.30.refs_0_, bf16[2,32,3072]{2,1,0:T(8,128)(2,1)S(1)} %slice_select_fusion.refs_1_, bf16[2,32,3072]{2,1,0:T(8,128)(2,1)S(1)} %collective-permute-done.13.refs_2_, ...), custom_call_target="tpu_custom_call" | custom-call | flops 1024 | bytes 1024 | tf_op jit(solution)/shard_map/pallas_call | solution.py:22
  179.8 0.6 collective-permute-start.17
  180.3 2.1 shard_map.62.refs_0_.refs_1_
  182.4 0.1 collective-permute-start.18
  182.5 0.9 collective-permute-done.17.refs_2_.refs_5_
  183.4 0.8 shard_map.63.refs_0_
  184.1 1.3 collective-permute-start.22
  185.4 2.2 collective-permute-start.10
  187.6 0.7 collective-permute-start.11
  188.4 0.4 collective-permute-start.12
  188.8 19.4 %shard_map.64 = (f32[2,32,3072]{2,1,0:T(8,128)S(1)}, bf16[2,32,3072]{2,1,0:T(8,128)(2,1)S(1)}, bf16[2,32,3072]{2,1,0:T(8,128)(2,1)S(1)}, bf16[2,32,3072]{2,1,0:T(8,128)(2,1)S(1)}) custom-call(bf16[128,6144]{1,0:T(8,128)(2,1)S(1)} %shard_map.63.refs_0_, bf16[128,6144]{1,0:T(8,128)(2,1)S(1)} %shard_map.62.refs_0_.refs_1_, ...), custom_call_target="tpu_custom_call" | custom-call | flops 1024 | bytes 1024 | tf_op jit(solution)/shard_map/pallas_call | solution.py:22
  208.2 12.5 %collective-permute-done.11.refs_2_ = bf16[2,32,3072]{2,1,0:T(8,128)(2,1)S(1)} collective-permute-done((bf16[2,32,3072]{2,1,0:T(8,128)(2,1)S(1)}, bf16[2,32,3072]{2,1,0:T(8,128)(2,1)S(1)}, u32[]{:S(2)}, u32[]{:S(2)}) %collective-permute-start.11) | collective-permute-done | bytes 393248 | tf_op jit(solution)/shard_map/ppermute | solution.py:180
  220.7 1.9 collective-permute-done.12.refs_3_
  222.6 2.1 shard_map.65.refs_0_.refs_2_
  224.7 0.9 collective-permute-start.23
  225.6 1.5 collective-permute-start.21
  227.1 1.9 collective-permute-start.20
  229.0 7.3 %collective-permute-done.19.refs_1_ = bf16[2,32,3072]{2,1,0:T(8,128)(2,1)S(1)} collective-permute-done((bf16[2,32,3072]{2,1,0:T(8,128)(2,1)S(1)}, bf16[2,32,3072]{2,1,0:T(8,128)(2,1)S(1)}, u32[]{:S(2)}, u32[]{:S(2)}) %collective-permute-start.19) | collective-permute-done | bytes 393248 | tf_op jit(solution)/shard_map/ppermute | solution.py:180
  236.3 19.4 %shard_map.66 = (f32[2,32,3072]{2,1,0:T(8,128)S(1)}, bf16[2,32,3072]{2,1,0:T(8,128)(2,1)S(1)}, bf16[2,32,3072]{2,1,0:T(8,128)(2,1)S(1)}, bf16[2,32,3072]{2,1,0:T(8,128)(2,1)S(1)}) custom-call(bf16[128,6144]{1,0:T(8,128)(2,1)S(1)} %shard_map.65.refs_0_.refs_2_, bf16[2,32,3072]{2,1,0:T(8,128)(2,1)S(1)} %collective-permute-done.19.refs_1_, ...), custom_call_target="tpu_custom_call" | custom-call | flops 1024 | bytes 1024 | tf_op jit(solution)/shard_map/pallas_call | solution.py:22
  255.7 9.1 %collective-permute-start.24 = (bf16[2,32,3072]{2,1,0:T(8,128)(2,1)S(1)}, bf16[2,32,3072]{2,1,0:T(8,128)(2,1)S(1)}, u32[]{:S(2)}, u32[]{:S(2)}) collective-permute-start(bf16[2,32,3072]{2,1,0:T(8,128)(2,1)S(1)} %get-tuple-element.38), channel_id=1, source_target_pairs={{0,4},{4,8},{8,12},{12,0},{1,5},{5,9},{9,13},{13,1},{2,6},{6,10},{... | collective-permute-start | bytes 1179656 | tf_op jit(solution)/shard_map/ppermute | solution.py:180
  264.8 2.5 collective-permute-start.25
  267.3 1.4 collective-permute-start.26
  268.6 20.0 %collective-permute-done.24 = bf16[2,32,3072]{2,1,0:T(8,128)(2,1)S(1)} collective-permute-done((bf16[2,32,3072]{2,1,0:T(8,128)(2,1)S(1)}, bf16[2,32,3072]{2,1,0:T(8,128)(2,1)S(1)}, u32[]{:S(2)}, u32[]{:S(2)}) %collective-permute-start.24) | collective-permute-done | bytes 393248 | tf_op jit(solution)/shard_map/ppermute | solution.py:180
  288.7 8.4 %collective-permute-done.25 = bf16[2,32,3072]{2,1,0:T(8,128)(2,1)S(1)} collective-permute-done((bf16[2,32,3072]{2,1,0:T(8,128)(2,1)S(1)}, bf16[2,32,3072]{2,1,0:T(8,128)(2,1)S(1)}, u32[]{:S(2)}, u32[]{:S(2)}) %collective-permute-start.25) | collective-permute-done | bytes 393248 | tf_op jit(solution)/shard_map/ppermute | solution.py:180
  297.1 5.0 %collective-permute-done.26 = bf16[2,32,3072]{2,1,0:T(8,128)(2,1)S(1)} collective-permute-done((bf16[2,32,3072]{2,1,0:T(8,128)(2,1)S(1)}, bf16[2,32,3072]{2,1,0:T(8,128)(2,1)S(1)}, u32[]{:S(2)}, u32[]{:S(2)}) %collective-permute-start.26) | collective-permute-done | bytes 393248 | tf_op jit(solution)/shard_map/ppermute | solution.py:180
  302.1 0.7 add_convert_fusion.2
  302.8 0.1 pad_maximum_fusion
  302.9 1.3 reverse_select_fusion
  (21 shorter events, 0.1 us)
Async XLA Ops:
  2.1 10.0 %collective-permute-start = (bf16[2,32,3072]{2,1,0:T(8,128)(2,1)S(1)}, bf16[2,32,3072]{2,1,0:T(8,128)(2,1)S(1)}, u32[]{:S(2)}, u32[]{:S(2)}) collective-permute-start(bf16[2,32,3072]{2,1,0:T(8,128)(2,1)S(1)} %slice.46.refs_1_), channel_id=1, source_target_pairs={{4,0},{8,4},{12,8},{0,12},{5,1},{9,5},{13,9},{1,13},{6,2},{10,6},{... | collective-permute-start | bytes 1179656 | tf_op jit(solution)/shard_map/ppermute | solution.py:137
  2.3 27.3 %collective-permute-start.1 = (bf16[2,32,3072]{2,1,0:T(8,128)(2,1)S(1)}, bf16[2,32,3072]{2,1,0:T(8,128)(2,1)S(1)}, u32[]{:S(2)}, u32[]{:S(2)}) collective-permute-start(bf16[2,32,3072]{2,1,0:T(8,128)(2,1)S(1)} %slice.46.refs_1_), channel_id=1, source_target_pairs={{8,0},{12,4},{0,8},{4,12},{9,1},{13,5},{1,9},{5,13},{10,2},{14,6},... | collective-permute-start | bytes 1179656 | tf_op jit(solution)/shard_map/ppermute | solution.py:137
  4.6 33.4 %collective-permute-start.2 = (bf16[2,32,3072]{2,1,0:T(8,128)(2,1)S(1)}, bf16[2,32,3072]{2,1,0:T(8,128)(2,1)S(1)}, u32[]{:S(2)}, u32[]{:S(2)}) collective-permute-start(bf16[2,32,3072]{2,1,0:T(8,128)(2,1)S(1)} %slice.46.refs_1_), channel_id=1, source_target_pairs={{12,0},{0,4},{4,8},{8,12},{13,1},{1,5},{5,9},{9,13},{14,2},{2,6},{... | collective-permute-start | bytes 1179656 | tf_op jit(solution)/shard_map/ppermute | solution.py:137
  58.5 4.4 %collective-permute-start.3 = (bf16[128,6144]{1,0:T(8,128)(2,1)S(1)}, bf16[128,6144]{1,0:T(8,128)(2,1)S(1)}, u32[]{:S(2)}, u32[]{:S(2)}) collective-permute-start(bf16[128,6144]{1,0:T(8,128)(2,1)S(1)} %get-tuple-element.23.refs_0_), channel_id=1, source_target_pairs={{0,1},{1,0},{2,3},{3,2},{4,5},{5,4},{6,7},{7,6},{8,9},{9,8},{10,11... | collective-permute-start | bytes 4718600 | tf_op jit(solution)/shard_map/ppermute | solution.py:149
  63.6 57.3 %collective-permute-start.7 = (bf16[128,6144]{1,0:T(8,128)(2,1)S(1)}, bf16[128,6144]{1,0:T(8,128)(2,1)S(1)}, u32[]{:S(2)}, u32[]{:S(2)}) collective-permute-start(bf16[128,6144]{1,0:T(8,128)(2,1)S(1)} %shard_map.56.refs_0_), channel_id=1, source_target_pairs={{0,2},{1,3},{2,0},{3,1},{4,6},{5,7},{6,4},{7,5},{8,10},{9,11},{10,... | collective-permute-start | bytes 4718600 | tf_op jit(solution)/shard_map/ppermute | solution.py:156
  63.9 11.1 %collective-permute-start.4 = (bf16[2,32,3072]{2,1,0:T(8,128)(2,1)S(1)}, bf16[2,32,3072]{2,1,0:T(8,128)(2,1)S(1)}, u32[]{:S(2)}, u32[]{:S(2)}) collective-permute-start(bf16[2,32,3072]{2,1,0:T(8,128)(2,1)S(1)} %slice_select_fusion.1.refs_0_.refs_2_), channel_id=1, source_target_pairs={{4,0},{8,4},{12,8},{0,12},{5,1},{9,5},{13,9},{1,13},{6,2},{10,6},{... | collective-permute-start | bytes 1179656 | tf_op jit(solution)/shard_map/ppermute | solution.py:137
  66.0 25.5 %collective-permute-start.5 = (bf16[2,32,3072]{2,1,0:T(8,128)(2,1)S(1)}, bf16[2,32,3072]{2,1,0:T(8,128)(2,1)S(1)}, u32[]{:S(2)}, u32[]{:S(2)}) collective-permute-start(bf16[2,32,3072]{2,1,0:T(8,128)(2,1)S(1)} %slice_select_fusion.1.refs_0_.refs_2_), channel_id=1, source_target_pairs={{8,0},{12,4},{0,8},{4,12},{9,1},{13,5},{1,9},{5,13},{10,2},{14,6},... | collective-permute-start | bytes 1179656 | tf_op jit(solution)/shard_map/ppermute | solution.py:137
  67.3 32.5 %collective-permute-start.6 = (bf16[2,32,3072]{2,1,0:T(8,128)(2,1)S(1)}, bf16[2,32,3072]{2,1,0:T(8,128)(2,1)S(1)}, u32[]{:S(2)}, u32[]{:S(2)}) collective-permute-start(bf16[2,32,3072]{2,1,0:T(8,128)(2,1)S(1)} %slice_select_fusion.1.refs_0_.refs_2_), channel_id=1, source_target_pairs={{12,0},{0,4},{4,8},{8,12},{13,1},{1,5},{5,9},{9,13},{14,2},{2,6},{... | collective-permute-start | bytes 1179656 | tf_op jit(solution)/shard_map/ppermute | solution.py:137
  101.1 19.9 %copy-start = (f32[6144]{0:T(1024)S(1)}, f32[6144]{0:T(1024)}, u32[]{:S(2)}) copy-start(f32[6144]{0:T(1024)} %param.7) | copy-start | bytes 73732
  120.4 7.5 %collective-permute-start.8 = (bf16[128,6144]{1,0:T(8,128)(2,1)S(1)}, bf16[128,6144]{1,0:T(8,128)(2,1)S(1)}, u32[]{:S(2)}, u32[]{:S(2)}) collective-permute-start(bf16[128,6144]{1,0:T(8,128)(2,1)S(1)} %get-tuple-element.25.refs_0_), channel_id=1, source_target_pairs={{0,1},{1,0},{2,3},{3,2},{4,5},{5,4},{6,7},{7,6},{8,9},{9,8},{10,11... | collective-permute-start | bytes 4718600 | tf_op jit(solution)/shard_map/ppermute | solution.py:149
  123.0 6.9 %collective-permute-start.9 = (bf16[128,6144]{1,0:T(8,128)(2,1)S(1)}, bf16[128,6144]{1,0:T(8,128)(2,1)S(1)}, u32[]{:S(2)}, u32[]{:S(2)}) collective-permute-start(bf16[128,6144]{1,0:T(8,128)(2,1)S(1)} %shard_map.58.refs_0_.refs_1_), channel_id=1, source_target_pairs={{0,1},{1,0},{2,3},{3,2},{4,5},{5,4},{6,7},{7,6},{8,9},{9,8},{10,11... | collective-permute-start | bytes 4718600 | tf_op jit(solution)/shard_map/ppermute | solution.py:165
  123.1 26.2 %collective-permute-start.13 = (bf16[2,32,3072]{2,1,0:T(8,128)(2,1)S(1)}, bf16[2,32,3072]{2,1,0:T(8,128)(2,1)S(1)}, u32[]{:S(2)}, u32[]{:S(2)}) collective-permute-start(bf16[2,32,3072]{2,1,0:T(8,128)(2,1)S(1)} %slice_select_fusion.refs_1_), channel_id=1, source_target_pairs={{4,0},{8,4},{12,8},{0,12},{5,1},{9,5},{13,9},{1,13},{6,2},{10,6},{... | collective-permute-start | bytes 1179656 | tf_op jit(solution)/shard_map/ppermute | solution.py:137
  126.6 25.5 %collective-permute-start.14 = (bf16[2,32,3072]{2,1,0:T(8,128)(2,1)S(1)}, bf16[2,32,3072]{2,1,0:T(8,128)(2,1)S(1)}, u32[]{:S(2)}, u32[]{:S(2)}) collective-permute-start(bf16[2,32,3072]{2,1,0:T(8,128)(2,1)S(1)} %slice_select_fusion.refs_1_), channel_id=1, source_target_pairs={{8,0},{12,4},{0,8},{4,12},{9,1},{13,5},{1,9},{5,13},{10,2},{14,6},... | collective-permute-start | bytes 1179656 | tf_op jit(solution)/shard_map/ppermute | solution.py:137
  126.6 33.9 %collective-permute-start.15 = (bf16[2,32,3072]{2,1,0:T(8,128)(2,1)S(1)}, bf16[2,32,3072]{2,1,0:T(8,128)(2,1)S(1)}, u32[]{:S(2)}, u32[]{:S(2)}) collective-permute-start(bf16[2,32,3072]{2,1,0:T(8,128)(2,1)S(1)} %slice_select_fusion.refs_1_), channel_id=1, source_target_pairs={{12,0},{0,4},{4,8},{8,12},{13,1},{1,5},{5,9},{9,13},{14,2},{2,6},{... | collective-permute-start | bytes 1179656 | tf_op jit(solution)/shard_map/ppermute | solution.py:137
  128.7 51.7 %collective-permute-start.16 = (bf16[128,6144]{1,0:T(8,128)(2,1)S(1)}, bf16[128,6144]{1,0:T(8,128)(2,1)S(1)}, u32[]{:S(2)}, u32[]{:S(2)}) collective-permute-start(bf16[128,6144]{1,0:T(8,128)(2,1)S(1)} %shard_map.59.refs_0_), channel_id=1, source_target_pairs={{0,2},{1,3},{2,0},{3,1},{4,6},{5,7},{6,4},{7,5},{8,10},{9,11},{10,... | collective-permute-start | bytes 4718600 | tf_op jit(solution)/shard_map/ppermute | solution.py:156
  179.8 3.6 %collective-permute-start.17 = (bf16[128,6144]{1,0:T(8,128)(2,1)S(1)}, bf16[128,6144]{1,0:T(8,128)(2,1)S(1)}, u32[]{:S(2)}, u32[]{:S(2)}) collective-permute-start(bf16[128,6144]{1,0:T(8,128)(2,1)S(1)} %get-tuple-element.31.refs_0_), channel_id=1, source_target_pairs={{0,1},{1,0},{2,3},{3,2},{4,5},{5,4},{6,7},{7,6},{8,9},{9,8},{10,11... | collective-permute-start | bytes 4718600 | tf_op jit(solution)/shard_map/ppermute | solution.py:149
  182.4 6.4 %collective-permute-start.18 = (bf16[128,6144]{1,0:T(8,128)(2,1)S(1)}, bf16[128,6144]{1,0:T(8,128)(2,1)S(1)}, u32[]{:S(2)}, u32[]{:S(2)}) collective-permute-start(bf16[128,6144]{1,0:T(8,128)(2,1)S(1)} %shard_map.62.refs_0_.refs_1_), channel_id=1, source_target_pairs={{0,1},{1,0},{2,3},{3,2},{4,5},{5,4},{6,7},{7,6},{8,9},{9,8},{10,11... | collective-permute-start | bytes 4718600 | tf_op jit(solution)/shard_map/ppermute | solution.py:165
  184.1 38.5 %collective-permute-start.22 = (bf16[128,6144]{1,0:T(8,128)(2,1)S(1)}, bf16[128,6144]{1,0:T(8,128)(2,1)S(1)}, u32[]{:S(2)}, u32[]{:S(2)}) collective-permute-start(bf16[128,6144]{1,0:T(8,128)(2,1)S(1)} %shard_map.63.refs_0_), channel_id=1, source_target_pairs={{0,2},{1,3},{2,0},{3,1},{4,6},{5,7},{6,4},{7,5},{8,10},{9,11},{10,... | collective-permute-start | bytes 4718600 | tf_op jit(solution)/shard_map/ppermute | solution.py:156
  185.4 22.8 %collective-permute-start.10 = (bf16[2,32,3072]{2,1,0:T(8,128)(2,1)S(1)}, bf16[2,32,3072]{2,1,0:T(8,128)(2,1)S(1)}, u32[]{:S(2)}, u32[]{:S(2)}) collective-permute-start(bf16[2,32,3072]{2,1,0:T(8,128)(2,1)S(1)} %get-tuple-element.28), channel_id=1, source_target_pairs={{0,4},{4,8},{8,12},{12,0},{1,5},{5,9},{9,13},{13,1},{2,6},{6,10},{... | collective-permute-start | bytes 1179656 | tf_op jit(solution)/shard_map/ppermute | solution.py:180
  187.6 33.1 %collective-permute-start.11 = (bf16[2,32,3072]{2,1,0:T(8,128)(2,1)S(1)}, bf16[2,32,3072]{2,1,0:T(8,128)(2,1)S(1)}, u32[]{:S(2)}, u32[]{:S(2)}) collective-permute-start(bf16[2,32,3072]{2,1,0:T(8,128)(2,1)S(1)} %get-tuple-element.29), channel_id=1, source_target_pairs={{0,8},{4,12},{8,0},{12,4},{1,9},{5,13},{9,1},{13,5},{2,10},{6,14},... | collective-permute-start | bytes 1179656 | tf_op jit(solution)/shard_map/ppermute | solution.py:180
  188.4 34.2 %collective-permute-start.12 = (bf16[2,32,3072]{2,1,0:T(8,128)(2,1)S(1)}, bf16[2,32,3072]{2,1,0:T(8,128)(2,1)S(1)}, u32[]{:S(2)}, u32[]{:S(2)}) collective-permute-start(bf16[2,32,3072]{2,1,0:T(8,128)(2,1)S(1)} %get-tuple-element.30.refs_0_), channel_id=1, source_target_pairs={{0,12},{4,0},{8,4},{12,8},{1,13},{5,1},{9,5},{13,9},{2,14},{6,2},{... | collective-permute-start | bytes 1179656 | tf_op jit(solution)/shard_map/ppermute | solution.py:180
  224.7 11.6 %collective-permute-start.23 = (bf16[128,6144]{1,0:T(8,128)(2,1)S(1)}, bf16[128,6144]{1,0:T(8,128)(2,1)S(1)}, u32[]{:S(2)}, u32[]{:S(2)}) collective-permute-start(bf16[128,6144]{1,0:T(8,128)(2,1)S(1)} %shard_map.65.refs_0_.refs_2_), channel_id=1, source_target_pairs={{0,1},{1,0},{2,3},{3,2},{4,5},{5,4},{6,7},{7,6},{8,9},{9,8},{10,11... | collective-permute-start | bytes 4718600 | tf_op jit(solution)/shard_map/ppermute | solution.py:165
  225.6 10.7 %collective-permute-start.19 = (bf16[2,32,3072]{2,1,0:T(8,128)(2,1)S(1)}, bf16[2,32,3072]{2,1,0:T(8,128)(2,1)S(1)}, u32[]{:S(2)}, u32[]{:S(2)}) collective-permute-start(bf16[2,32,3072]{2,1,0:T(8,128)(2,1)S(1)} %get-tuple-element.34), channel_id=1, source_target_pairs={{0,4},{4,8},{8,12},{12,0},{1,5},{5,9},{9,13},{13,1},{2,6},{6,10},{... | collective-permute-start | bytes 1179656 | tf_op jit(solution)/shard_map/ppermute | solution.py:180
  225.6 43.0 %collective-permute-start.21 = (bf16[2,32,3072]{2,1,0:T(8,128)(2,1)S(1)}, bf16[2,32,3072]{2,1,0:T(8,128)(2,1)S(1)}, u32[]{:S(2)}, u32[]{:S(2)}) collective-permute-start(bf16[2,32,3072]{2,1,0:T(8,128)(2,1)S(1)} %get-tuple-element.36.refs_0_), channel_id=1, source_target_pairs={{0,12},{4,0},{8,4},{12,8},{1,13},{5,1},{9,5},{13,9},{2,14},{6,2},{... | collective-permute-start | bytes 1179656 | tf_op jit(solution)/shard_map/ppermute | solution.py:180
  227.1 75.0 %copy-start.1 = (f32[3072]{0:T(1024)S(1)}, f32[3072]{0:T(1024)}, u32[]{:S(2)}) copy-start(f32[3072]{0:T(1024)} %param.9) | copy-start | bytes 36868
  227.1 41.6 %collective-permute-start.20 = (bf16[2,32,3072]{2,1,0:T(8,128)(2,1)S(1)}, bf16[2,32,3072]{2,1,0:T(8,128)(2,1)S(1)}, u32[]{:S(2)}, u32[]{:S(2)}) collective-permute-start(bf16[2,32,3072]{2,1,0:T(8,128)(2,1)S(1)} %get-tuple-element.35), channel_id=1, source_target_pairs={{0,8},{4,12},{8,0},{12,4},{1,9},{5,13},{9,1},{13,5},{2,10},{6,14},... | collective-permute-start | bytes 1179656 | tf_op jit(solution)/shard_map/ppermute | solution.py:180
  255.7 33.0 %collective-permute-start.24 = (bf16[2,32,3072]{2,1,0:T(8,128)(2,1)S(1)}, bf16[2,32,3072]{2,1,0:T(8,128)(2,1)S(1)}, u32[]{:S(2)}, u32[]{:S(2)}) collective-permute-start(bf16[2,32,3072]{2,1,0:T(8,128)(2,1)S(1)} %get-tuple-element.38), channel_id=1, source_target_pairs={{0,4},{4,8},{8,12},{12,0},{1,5},{5,9},{9,13},{13,1},{2,6},{6,10},{... | collective-permute-start | bytes 1179656 | tf_op jit(solution)/shard_map/ppermute | solution.py:180
  264.8 32.3 %collective-permute-start.25 = (bf16[2,32,3072]{2,1,0:T(8,128)(2,1)S(1)}, bf16[2,32,3072]{2,1,0:T(8,128)(2,1)S(1)}, u32[]{:S(2)}, u32[]{:S(2)}) collective-permute-start(bf16[2,32,3072]{2,1,0:T(8,128)(2,1)S(1)} %get-tuple-element.39), channel_id=1, source_target_pairs={{0,8},{4,12},{8,0},{12,4},{1,9},{5,13},{9,1},{13,5},{2,10},{6,14},... | collective-permute-start | bytes 1179656 | tf_op jit(solution)/shard_map/ppermute | solution.py:180
  267.3 34.8 %collective-permute-start.26 = (bf16[2,32,3072]{2,1,0:T(8,128)(2,1)S(1)}, bf16[2,32,3072]{2,1,0:T(8,128)(2,1)S(1)}, u32[]{:S(2)}, u32[]{:S(2)}) collective-permute-start(bf16[2,32,3072]{2,1,0:T(8,128)(2,1)S(1)} %get-tuple-element.40), channel_id=1, source_target_pairs={{0,12},{4,0},{8,4},{12,8},{1,13},{5,1},{9,5},{13,9},{2,14},{6,2},{... | collective-permute-start | bytes 1179656 | tf_op jit(solution)/shard_map/ppermute | solution.py:180
